TPU v7x, 512 devices: a whole 4x8x8 slice. The times are simulated.
512 devices in a mesh: ctx: 64 (over y, z), head: 8 (over x, core).
Axes of the slice: x: 4, y: 8, z: 8, core: 2. Of those that a mesh axis runs over, the one named last changes fastest.
Arguments:
- qkv_raw: bfloat16 [8192, 3, 2048], P('ctx', None, 'head'), may hold values from -6 to 6
- positions: int32 [8192], P('ctx'), may hold values from 0 to 8191, as said below
- filter_taps: float32 [3, 3, 2048], P(None, None, 'head'), may hold values from -1.2 to 1.2
- grad_out: bfloat16 [8192, 2048], P(('ctx', 'head')), may hold values from -6 to 6
Outputs:
- attn_out: bfloat16 [8192, 2048], P('ctx', 'head')
- qkv_grad: bfloat16 [8192, 3, 2048], P('ctx', None, 'head')
Inputs may be any that keep to these rules, and one draw needn't show every extreme that they name: Rows 128 d to 128 d + 127 hold, in increasing order, the positions of group c and then those of group 2 * 64 - 1 - c, each group being 64 consecutive positions, where c = (d + r) mod 64 with one r for the whole array; every position appears once.
All inputs are finite; a program needn't handle non-finite values.
Results may differ from a plain program's by a relative error of at most 0.03.
Values may be sent and summed in bfloat16 or wider, within the bound.
A program may use at most 64 MiB of HBM per device.

v0:
```python
import math
import jax
import jax.numpy as jnp
from jax import lax
from jax.sharding import PartitionSpec as P

HEAD_SIZE = 128
NEG_LARGE = -1e30


def extended_2(cells, sides, width):
    for axis, dim in sides:
        count = lax.axis_size(axis)
        head = lax.slice_in_dim(cells, 0, width, axis=dim)
        tail = lax.slice_in_dim(cells, cells.shape[dim] - width, cells.shape[dim], axis=dim)
        cells = jnp.concatenate(
            [
                lax.ppermute(tail, axis, [(i, (i + 1) % count) for i in range(count)]),
                cells,
                lax.ppermute(head, axis, [((i + 1) % count, i) for i in range(count)]),
            ],
            axis=dim,
        )
    return cells


def featurize(group_rows, prior_rows, filter_taps):
    rim_width = prior_rows.shape[0]
    row_count = group_rows.shape[0]
    extended = jnp.concatenate([prior_rows, group_rows], axis=0).astype(jnp.float32)
    result = jnp.zeros(group_rows.shape, jnp.float32)
    for tap_index in range(filter_taps.shape[1]):
        begin = rim_width - tap_index
        result = result + filter_taps[None, :, tap_index, :] * extended[begin : begin + row_count]
    return result


def unfeaturize(grad_rows, next_rows, filter_taps):
    row_count = grad_rows.shape[0]
    extended = jnp.concatenate([grad_rows, next_rows], axis=0)
    result = jnp.zeros(grad_rows.shape, jnp.float32)
    for tap_index in range(filter_taps.shape[1]):
        result = (
            result
            + filter_taps[None, :, tap_index, :] * extended[tap_index : tap_index + row_count]
        )
    return result


def locate_rows(first_row, row_count, group_len, pair_here, device_here, pair_count):
    row_ids = first_row + jnp.arange(row_count, dtype=jnp.int32)
    device_ids = row_ids // group_len
    pair_ids = (device_ids + pair_here - device_here) % pair_count
    offsets = row_ids % group_len
    early_pos = pair_ids * group_len + offsets
    late_pos = (2 * pair_count - 1 - pair_ids) * group_len + offsets
    return (early_pos, late_pos)


def split_product(left_wide, key_rows):
    high_part = left_wide.astype(jnp.bfloat16)
    rest_one = left_wide - high_part.astype(jnp.float32)
    middle_part = rest_one.astype(jnp.bfloat16)
    low_part = (rest_one - middle_part.astype(jnp.float32)).astype(jnp.bfloat16)
    total = jnp.einsum("hqk,khd->qhd", high_part, key_rows, preferred_element_type=jnp.float32)
    total = total + jnp.einsum(
        "hqk,khd->qhd", middle_part, key_rows, preferred_element_type=jnp.float32
    )
    return total + jnp.einsum(
        "hqk,khd->qhd", low_part, key_rows, preferred_element_type=jnp.float32
    )


def fresh_forward(row_count, head_count, head_size):
    return (
        jnp.full((head_count, row_count), NEG_LARGE, jnp.float32),
        jnp.zeros((head_count, row_count), jnp.float32),
        jnp.zeros((row_count, head_count, head_size), jnp.float32),
        jnp.zeros((row_count, head_count, head_size), jnp.float32),
        jnp.zeros((row_count, head_count, head_size), jnp.float32),
    )


def forward_update(
    carry_state, queries, query_pos, out_grads, key_rows, value_rows, key_pos, scaling
):
    running_max, running_sum, out_sum, weighted, plain_sum = carry_state
    scores = (
        jnp.einsum("qhd,khd->hqk", queries, key_rows, preferred_element_type=jnp.float32) * scaling
    )
    allowed = (key_pos[None, :] <= query_pos[:, None])[None]
    masked = jnp.where(allowed, scores, NEG_LARGE)
    new_max = jnp.maximum(running_max, jnp.max(masked, axis=2))
    factor = jnp.exp(running_max - new_max)
    weights = jnp.where(allowed, jnp.exp(masked - new_max[:, :, None]), 0.0)
    running_sum = running_sum * factor + jnp.sum(weights, axis=2)
    rescale = jnp.transpose(factor)[:, :, None]
    out_sum = out_sum * rescale + jnp.einsum(
        "hqk,khd->qhd", weights.astype(jnp.bfloat16), value_rows, preferred_element_type=jnp.float32
    )
    slopes = jnp.einsum("qhd,khd->hqk", out_grads, value_rows, preferred_element_type=jnp.float32)
    weighted = weighted * rescale + split_product(weights * slopes, key_rows)
    plain_sum = plain_sum * rescale + split_product(weights, key_rows)
    return (new_max, running_sum, out_sum, weighted, plain_sum)


def forward_finish(carry_state, out_grads, scaling):
    running_max, running_sum, out_sum, weighted, plain_sum = carry_state
    inverse = jnp.transpose(1.0 / running_sum)[:, :, None]
    attn = (out_sum * inverse).astype(jnp.bfloat16)
    log_total = jnp.transpose(running_max + jnp.log(running_sum))
    delta = jnp.sum(out_grads.astype(jnp.float32) * attn.astype(jnp.float32), axis=2)
    query_grad = scaling * (weighted - delta[:, :, None] * plain_sum) * inverse
    return (attn, log_total, delta, query_grad)


def forward_absorber(queries, out_grads, query_pos, locate, scaling):
    group_len = queries.shape[0] // 2
    head_count = queries.shape[1]
    head_size = queries.shape[2]

    def absorb(carried, block_in, first_row):
        key_block, value_block = block_in
        row_count = key_block.shape[1]
        step_rows = math.gcd(row_count, 256)

        def inner(step_index, state_pair):
            begin = step_index * step_rows
            key_part = lax.dynamic_slice_in_dim(key_block, begin, step_rows, 1).reshape(
                2, step_rows, head_count, head_size
            )
            value_part = lax.dynamic_slice_in_dim(value_block, begin, step_rows, 1).reshape(
                2, step_rows, head_count, head_size
            )
            early_pos, late_pos = locate(begin, step_rows)
            early_state, late_state = state_pair
            keys_both = key_part.reshape(2 * step_rows, head_count, head_size)
            values_both = value_part.reshape(2 * step_rows, head_count, head_size)
            pos_both = jnp.concatenate([early_pos, late_pos])
            late_state = forward_update(
                late_state,
                queries[group_len:],
                query_pos[group_len:],
                out_grads[group_len:],
                keys_both,
                values_both,
                pos_both,
                scaling,
            )
            early_state = forward_update(
                early_state,
                queries[:group_len],
                query_pos[:group_len],
                out_grads[:group_len],
                keys_both,
                values_both,
                pos_both,
                scaling,
            )
            return (early_state, late_state)

        return lax.fori_loop(0, row_count // step_rows, inner, carried)

    return absorb


def backward_update(
    grads_pair,
    key_rows,
    value_rows,
    key_pos,
    queries,
    out_grads,
    log_rows,
    delta_rows,
    query_pos,
    scaling,
):
    key_grad, value_grad = grads_pair
    scores = (
        jnp.einsum("qhd,khd->hqk", queries, key_rows, preferred_element_type=jnp.float32) * scaling
    )
    allowed = (key_pos[None, :] <= query_pos[:, None])[None]
    shifted = jnp.where(allowed, scores - jnp.transpose(log_rows)[:, :, None], NEG_LARGE)
    probs = jnp.where(allowed, jnp.exp(shifted), 0.0)
    value_grad = value_grad + jnp.einsum(
        "hqk,qhd->khd", probs.astype(jnp.bfloat16), out_grads, preferred_element_type=jnp.float32
    )
    slopes = jnp.einsum("qhd,khd->hqk", out_grads, value_rows, preferred_element_type=jnp.float32)
    dscores = (probs * (slopes - jnp.transpose(delta_rows)[:, :, None])).astype(jnp.bfloat16)
    key_grad = key_grad + jnp.einsum(
        "hqk,qhd->khd", dscores, queries, preferred_element_type=jnp.float32
    )
    return (key_grad, value_grad)


def backward_absorber(key_rows, value_rows, key_pos, locate, scaling):
    group_len = key_rows.shape[0] // 2
    head_count = key_rows.shape[1]
    head_size = key_rows.shape[2]

    def absorb(carried, block_in, first_row):
        query_block, grad_block, log_block, delta_block = block_in
        row_count = query_block.shape[1]
        step_rows = math.gcd(row_count, 256)

        def inner(step_index, grads_now):
            begin = step_index * step_rows
            query_part = lax.dynamic_slice_in_dim(query_block, begin, step_rows, 1).reshape(
                2, step_rows, head_count, head_size
            )
            grad_part = lax.dynamic_slice_in_dim(grad_block, begin, step_rows, 1).reshape(
                2, step_rows, head_count, head_size
            )
            log_part = lax.dynamic_slice_in_dim(log_block, begin, step_rows, 1)
            delta_part = lax.dynamic_slice_in_dim(delta_block, begin, step_rows, 1)
            early_pos, late_pos = locate(begin, step_rows)
            early_grads, late_grads = grads_now
            query_both = query_part.reshape(2 * step_rows, head_count, head_size)
            grad_both = grad_part.reshape(2 * step_rows, head_count, head_size)
            log_both = log_part.reshape(2 * step_rows, head_count)
            delta_both = delta_part.reshape(2 * step_rows, head_count)
            pos_both = jnp.concatenate([early_pos, late_pos])
            early_grads = backward_update(
                early_grads,
                key_rows[:group_len],
                value_rows[:group_len],
                key_pos[:group_len],
                query_both,
                grad_both,
                log_both,
                delta_both,
                pos_both,
                scaling,
            )
            late_grads = backward_update(
                late_grads,
                key_rows[group_len:],
                value_rows[group_len:],
                key_pos[group_len:],
                query_both,
                grad_both,
                log_both,
                delta_both,
                pos_both,
                scaling,
            )
            return (early_grads, late_grads)

        return lax.fori_loop(0, row_count // step_rows, inner, carried)

    return absorb


def local(qkv_raw, positions, filter_taps, grad_out):
    row_total = positions.shape[0]
    group_len = row_total // 2
    rim_width = filter_taps.shape[1] - 1
    channels = qkv_raw.shape[2]
    head_size = HEAD_SIZE
    head_count = channels // head_size
    scaling = 1.0 / math.sqrt(head_size)
    pair_count = lax.axis_size("ctx")
    device_here = lax.axis_index("ctx")
    pair_here = positions[0] // group_len

    def locate(first_row, row_count):
        return locate_rows(first_row, row_count, group_len, pair_here, device_here, pair_count)

    out_grads = lax.all_to_all(grad_out, "head", split_axis=1, concat_axis=0, tiled=True)
    early_rows = qkv_raw[:group_len]
    late_rows = qkv_raw[group_len:]
    early_tail = early_rows[group_len - rim_width :]
    late_tail = late_rows[group_len - rim_width :]
    tails = extended_2(jnp.concatenate([late_tail, early_tail], axis=0), (("ctx", 0),), rim_width)
    from_left = tails[:rim_width]
    from_right = tails[tails.shape[0] - rim_width :]
    early_prior = jnp.where(pair_here == 0, jnp.zeros_like(from_left), from_left)
    late_prior = jnp.where(pair_here == pair_count - 1, early_tail, from_right)
    featured = jnp.concatenate(
        [
            featurize(early_rows, early_prior, filter_taps),
            featurize(late_rows, late_prior, filter_taps),
        ],
        axis=0,
    ).astype(jnp.bfloat16)
    query_rows = featured[:, 0]
    key_rows = featured[:, 1]
    value_rows = featured[:, 2]
    col_first = 0 * head_size
    col_last = col_first + head_count * head_size
    width_now = col_last - col_first
    query_heads = query_rows.reshape(row_total, head_count, head_size)
    grad_heads = out_grads.reshape(row_total, head_count, head_size)
    initial = (
        fresh_forward(group_len, head_count, head_size),
        fresh_forward(group_len, head_count, head_size),
    )
    absorb = forward_absorber(query_heads, grad_heads, positions, locate, scaling)
    early_state, late_state = absorb(
        initial,
        (
            lax.all_gather(key_rows.reshape(2, group_len, width_now), "ctx", axis=1, tiled=True),
            lax.all_gather(value_rows.reshape(2, group_len, width_now), "ctx", axis=1, tiled=True),
        ),
        jnp.int32(0),
    )
    early_out = forward_finish(early_state, grad_heads[:group_len], scaling)
    late_out = forward_finish(late_state, grad_heads[group_len:], scaling)
    attn = jnp.concatenate([early_out[0], late_out[0]], axis=0)
    log_total = jnp.concatenate([early_out[1], late_out[1]], axis=0)
    delta = jnp.concatenate([early_out[2], late_out[2]], axis=0)
    query_grad = jnp.concatenate([early_out[3], late_out[3]], axis=0)
    absorb_back = backward_absorber(
        key_rows.reshape(row_total, head_count, head_size),
        value_rows.reshape(row_total, head_count, head_size),
        positions,
        locate,
        scaling,
    )
    zero_grads = (
        jnp.zeros((group_len, head_count, head_size), jnp.float32),
        jnp.zeros((group_len, head_count, head_size), jnp.float32),
    )
    early_grads, late_grads = absorb_back(
        (zero_grads, zero_grads),
        (
            lax.all_gather(
                query_rows.reshape(2, group_len, width_now).astype(jnp.float32),
                "ctx",
                axis=1,
                tiled=True,
            ).astype(jnp.bfloat16),
            lax.all_gather(
                out_grads.reshape(2, group_len, width_now).astype(jnp.float32),
                "ctx",
                axis=1,
                tiled=True,
            ).astype(jnp.bfloat16),
            lax.all_gather(log_total.reshape(2, group_len, head_count), "ctx", axis=1, tiled=True),
            lax.all_gather(delta.reshape(2, group_len, head_count), "ctx", axis=1, tiled=True),
        ),
        jnp.int32(0),
    )
    key_grad = scaling * jnp.concatenate([early_grads[0], late_grads[0]], axis=0)
    value_grad = jnp.concatenate([early_grads[1], late_grads[1]], axis=0)
    results = [(attn, query_grad, key_grad, value_grad)]
    attn_all = jnp.concatenate([entry[0] for entry in results], axis=1).reshape(row_total, channels)
    query_grad_all = jnp.concatenate([entry[1] for entry in results], axis=1).reshape(
        row_total, channels
    )
    key_grad_all = jnp.concatenate([entry[2] for entry in results], axis=1).reshape(
        row_total, channels
    )
    value_grad_all = jnp.concatenate([entry[3] for entry in results], axis=1).reshape(
        row_total, channels
    )
    post_grads = jnp.stack([query_grad_all, key_grad_all, value_grad_all], axis=1)
    early_head = post_grads[:rim_width]
    late_head = post_grads[group_len : group_len + rim_width]
    heads_rim = extended_2(
        jnp.concatenate([early_head, late_head], axis=0), (("ctx", 0),), rim_width
    )
    grad_left = heads_rim[:rim_width]
    grad_right = heads_rim[heads_rim.shape[0] - rim_width :]
    early_next = jnp.where(pair_here == pair_count - 1, late_head, grad_right)
    late_next = jnp.where(pair_here == 0, jnp.zeros_like(grad_left), grad_left)
    raw_grads = jnp.concatenate(
        [
            unfeaturize(post_grads[:group_len], early_next, filter_taps),
            unfeaturize(post_grads[group_len:], late_next, filter_taps),
        ],
        axis=0,
    )
    return (attn_all, raw_grads.astype(jnp.bfloat16))


def solution(mesh):
    in_specs = (P("ctx", None, "head"), P("ctx"), P(None, None, "head"), P(("ctx", "head"), None))
    out_specs = (P("ctx", "head"), P("ctx", None, "head"))
    return jax.shard_map(local, mesh=mesh, in_specs=in_specs, out_specs=out_specs, check_vma=False)
```

profile of v0, /device:TPU:4, one launch (start us, length us, event | category | flops | bytes accessed | tf_op | source)
XLA Modules:
  0.0 526.5 jit_solution(4368539386016358668)
XLA Ops:
  7.9 13.8 %collective-permute-start.1 = (bf16[2,3,256]{2,0,1:T(2,128)(2,1)S(1)}, bf16[2,3,256]{2,0,1:T(2,128)(2,1)S(1)}, u32[]{:S(2)}, u32[]{:S(2)}) collective-permute-start(bf16[2,3,256]{2,0,1:T(2,128)(2,1)S(1)} %slice.223), channel_id=1, source_target_pairs={{8,0},{16,8},{24,16},{32,24},{40,32},{48,40},{56,48},{64,56},{72,6... | collective-permute-start | bytes 9224 | tf_op jit(solution)/shard_map/ppermute | solution.py:20
  26.9 1.9 collective-permute-start
  28.9 6.8 %collective-permute-done = bf16[2,3,256]{2,0,1:T(2,128)(2,1)S(1)} collective-permute-done((bf16[2,3,256]{2,0,1:T(2,128)(2,1)S(1)}, bf16[2,3,256]{2,0,1:T(2,128)(2,1)S(1)}, u32[]{:S(2)}, u32[]{:S(2)}) %collective-permute-start) | collective-permute-done | bytes 3104 | tf_op jit(solution)/shard_map/ppermute | solution.py:18
  38.1 1.5 copy.311
  39.6 4.8 all-to-all-start
  48.1 68.9 %all-gather.5.cloned.1.call-done = bf16[2,4096,256]{2,1,0:T(8,128)(2,1)} async-done(((bf16[2,64,256]{2,1,0:T(8,128)(2,1)}), bf16[2,4096,256]{2,1,0:T(8,128)(2,1)}) %all-gather.5.cloned.1.call-update) | async-done | bytes 4194320 | tf_op jit(solution)/shard_map/all_gather | solution.py:303
  117.0 87.5 %all-gather.7.cloned.1.call-done = bf16[2,4096,256]{2,1,0:T(8,128)(2,1)} async-done(((bf16[2,64,256]{2,1,0:T(8,128)(2,1)}), bf16[2,4096,256]{2,1,0:T(8,128)(2,1)}) %all-gather.7.cloned.1.call-update) | async-done | bytes 4194320 | tf_op jit(solution)/shard_map/all_gather | solution.py:304
  204.5 114.2 %while.56 = (s32[]{:T(128)}, f32[2,64]{1,0:T(2,128)S(1)}, f32[2,64]{1,0:T(2,128)S(1)}, f32[64,2,128]{2,0,1:T(8,128)S(1)}, f32[64,2,128]{2,0,1:T(8,128)S(1)}, /*i...) while((s32[]{:T(128)}, f32[2,64]{1,0:T(2,128)S(1)}, ...), condition=%wide.region_5.6_spmd.clone, body=%wide.region_0.5_spmd.clone.sunk | while | flops 308006656 | bytes 15106853 | solution.py:162
  206.9 1.0 constant_dynamic-slice_fusion.8
  211.7 1.0 constant_dynamic-slice_fusion.7
  214.1 1.0 constant_dynamic-slice_fusion.8
  218.8 1.0 constant_dynamic-slice_fusion.7
  221.2 1.0 constant_dynamic-slice_fusion.8
  225.9 1.0 constant_dynamic-slice_fusion.7
  228.3 1.0 constant_dynamic-slice_fusion.8
  233.1 1.0 constant_dynamic-slice_fusion.7
  235.5 1.0 constant_dynamic-slice_fusion.8
  240.2 1.0 constant_dynamic-slice_fusion.7
  242.6 1.0 constant_dynamic-slice_fusion.8
  247.3 1.0 constant_dynamic-slice_fusion.7
  249.8 1.0 constant_dynamic-slice_fusion.8
  254.5 1.0 constant_dynamic-slice_fusion.7
  256.9 1.0 constant_dynamic-slice_fusion.8
  261.6 1.0 constant_dynamic-slice_fusion.7
  264.0 1.0 constant_dynamic-slice_fusion.8
  268.8 1.0 constant_dynamic-slice_fusion.7
  271.2 1.0 constant_dynamic-slice_fusion.8
  275.9 1.0 constant_dynamic-slice_fusion.7
  278.3 1.0 constant_dynamic-slice_fusion.8
  283.1 1.0 constant_dynamic-slice_fusion.7
  285.5 1.0 constant_dynamic-slice_fusion.8
  290.2 1.0 constant_dynamic-slice_fusion.7
  292.6 1.0 constant_dynamic-slice_fusion.8
  297.4 1.0 constant_dynamic-slice_fusion.7
  299.8 1.0 constant_dynamic-slice_fusion.8
  304.5 1.0 constant_dynamic-slice_fusion.7
  306.9 1.0 constant_dynamic-slice_fusion.8
  311.6 1.0 constant_dynamic-slice_fusion.7
  314.0 1.0 constant_dynamic-slice_fusion.8
  320.3 66.3 %all_gather.23 = f32[2,4096,2]{2,0,1:T(2,128)} all-gather(f32[2,64,2]{2,0,1:T(2,128)S(1)} %copy.224), channel_id=1, replica_groups=mesh['ctx'=64,'head'=8] {'ctx'}, dimensions={1}, use_global_device_ids=true | all-gather | bytes 66560 | tf_op jit(solution)/shard_map/all_gather | solution.py:341
  386.6 5.2 copy.228
  392.1 56.2 %all_gather.21 = f32[2,4096,2]{2,0,1:T(2,128)} all-gather(f32[2,64,2]{2,0,1:T(2,128)S(1)} %copy.221), channel_id=1, replica_groups=mesh['ctx'=64,'head'=8] {'ctx'}, dimensions={1}, use_global_device_ids=true | all-gather | bytes 66560 | tf_op jit(solution)/shard_map/all_gather | solution.py:340
  448.3 5.1 copy.226
  454.2 49.3 %while.57 = (s32[]{:T(128)}, f32[64,2,128]{2,0,1:T(8,128)S(1)}, f32[64,2,128]{2,0,1:T(8,128)S(1)}, f32[64,2,128]{2,0,1:T(8,128)S(1)}, f32[64,2,128]{2,0,1:T(8,12...) while((s32[]{:T(128)}, f32[64,2,128]{2,0,1:T(8,128)S(1)}, ...), condition=%wide.region_9.10_spmd.clone, body=%wide.region_8.9_spmd.clone.sunk | while | flops 135473152 | bytes 6612724 | solution.py:250
  454.2 1.1 constant_dynamic-slice_fusion.9
  457.3 1.1 constant_dynamic-slice_fusion.9
  460.4 1.1 constant_dynamic-slice_fusion.9
  463.5 1.1 constant_dynamic-slice_fusion.9
  466.6 1.1 constant_dynamic-slice_fusion.9
  469.7 1.1 constant_dynamic-slice_fusion.9
  472.7 1.1 constant_dynamic-slice_fusion.9
  475.8 1.1 constant_dynamic-slice_fusion.9
  478.9 1.1 constant_dynamic-slice_fusion.9
  482.0 1.1 constant_dynamic-slice_fusion.9
  485.1 1.1 constant_dynamic-slice_fusion.9
  488.2 1.1 constant_dynamic-slice_fusion.9
  491.3 1.1 constant_dynamic-slice_fusion.9
  494.3 1.1 constant_dynamic-slice_fusion.9
  497.4 1.1 constant_dynamic-slice_fusion.9
  500.5 1.1 constant_dynamic-slice_fusion.9
  504.1 4.6 collective-permute-start.2
  508.7 1.3 collective-permute-done.2
  510.0 2.1 collective-permute-start.3
  512.2 6.9 %collective-permute-done.3 = f32[2,3,256]{2,0,1:T(2,128)S(1)} collective-permute-done((f32[2,3,256]{2,0,1:T(2,128)S(1)}, f32[2,3,256]{2,0,1:T(2,128)S(1)}, u32[]{:S(2)}, u32[]{:S(2)}) %collective-permute-start.3) | collective-permute-done | bytes 6176 | tf_op jit(solution)/shard_map/ppermute | solution.py:18
  (843 shorter events, 124.2 us)
Async XLA Ops:
  7.2 197.4 %copy-start.1 = (s32[128]{0:T(128)S(1)}, s32[128]{0:T(128)}, u32[]{:S(2)}) copy-start(s32[128]{0:T(128)} %param.9) | copy-start | bytes 1540
  7.2 109.8 %all-gather.5.cloned.1.call-start = ((), (), s32[]{:S(2)}) async-start(), calls=%async_computation.1 | async-start | bytes 4259840 | tf_op jit(solution)/shard_map/all_gather | solution.py:303
  7.9 18.3 %collective-permute-start.1 = (bf16[2,3,256]{2,0,1:T(2,128)(2,1)S(1)}, bf16[2,3,256]{2,0,1:T(2,128)(2,1)S(1)}, u32[]{:S(2)}, u32[]{:S(2)}) collective-permute-start(bf16[2,3,256]{2,0,1:T(2,128)(2,1)S(1)} %slice.223), channel_id=1, source_target_pairs={{8,0},{16,8},{24,16},{32,24},{40,32},{48,40},{56,48},{64,56},{72,6... | collective-permute-start | bytes 9224 | tf_op jit(solution)/shard_map/ppermute | solution.py:20
  26.9 8.8 %collective-permute-start = (bf16[2,3,256]{2,0,1:T(2,128)(2,1)S(1)}, bf16[2,3,256]{2,0,1:T(2,128)(2,1)S(1)}, u32[]{:S(2)}, u32[]{:S(2)}) collective-permute-start(bf16[2,3,256]{2,0,1:T(2,128)(2,1)S(1)} %get-tuple-element.1180), channel_id=1, source_target_pairs={{0,8},{8,16},{16,24},{24,32},{32,40},{40,48},{48,56},{56,64},{64,7... | collective-permute-start | bytes 9224 | tf_op jit(solution)/shard_map/ppermute | solution.py:18
  36.6 167.9 %all-gather.7.cloned.1.call-start = ((), (), s32[]{:S(2)}) async-start(), calls=%async_computation.2 | async-start | bytes 4259840 | tf_op jit(solution)/shard_map/all_gather | solution.py:304
  37.4 416.8 %all-gather.9.cloned.1.call-start = ((), (), s32[]{:S(2)}) async-start(), calls=%async_computation.3 | async-start | bytes 4259840 | tf_op jit(solution)/shard_map/all_gather | solution.py:328
  39.6 7.9 %all-to-all-start = ((bf16[16,8,256]{2,0,1:T(8,128)(2,1)}), bf16[16,8,256]{2,0,1:T(8,128)(2,1)S(1)}, u32[]{:S(2)}, u32[]{:S(2)}) async-start(bf16[16,8,256]{2,0,1:T(8,128)(2,1)} %bitcast.116), calls=%async_computation | async-start | bytes 131072 | tf_op jit(solution)/shard_map/all_to_all | solution.py:270
  44.4 409.8 %all-gather.11.cloned.1.call-start = ((), (), s32[]{:S(2)}) async-start(), calls=%async_computation.4 | async-start | bytes 4259840 | tf_op jit(solution)/shard_map/all_gather | solution.py:334
  47.5 0.6 copy-start
  504.1 5.9 %collective-permute-start.2 = (f32[2,3,256]{2,0,1:T(2,128)S(1)}, f32[2,3,256]{2,0,1:T(2,128)S(1)}, u32[]{:S(2)}, u32[]{:S(2)}) collective-permute-start(f32[2,3,256]{2,0,1:T(2,128)S(1)} %pad_maximum_fusion.8), channel_id=1, source_target_pairs={{8,0},{16,8},{24,16},{32,24},{40,32},{48,40},{56,48},{64,56},{72,6... | collective-permute-start | bytes 18440 | tf_op jit(solution)/shard_map/ppermute | solution.py:20
  510.0 9.1 %collective-permute-start.3 = (f32[2,3,256]{2,0,1:T(2,128)S(1)}, f32[2,3,256]{2,0,1:T(2,128)S(1)}, u32[]{:S(2)}, u32[]{:S(2)}) collective-permute-start(f32[2,3,256]{2,0,1:T(2,128)S(1)} %get-tuple-element.1145), channel_id=1, source_target_pairs={{0,8},{8,16},{16,24},{24,32},{32,40},{40,48},{48,56},{56,64},{64,7... | collective-permute-start | bytes 18440 | tf_op jit(solution)/shard_map/ppermute | solution.py:18
Sparse Core Ops, SparseCore 0:
  36.8 80.2 all-gather.4
  120.7 83.8 all-gather.6
  207.6 84.1 all-gather.8
  294.7 92.4 all-gather.10
where the time goes:
time: 529 us; the launch traced here: 526 us
  waiting for transfers between devices  173 us (33%)
  blocking collectives  123 us (23%)
  matrix products  91.4 us (17%)
  local copies, waits for them, and re-layouts  75.1 us (14%)
  starting transfers between devices  27.4 us (5%)
  between operations  16.8 us (3%)
  other arithmetic  15.2 us (3%)
    all_gather x1, waiting for transfers between devices, local(): lax.all_gather(value_rows.reshape(2, group_len, width_now), 'ctx', axis=1...  87.5 us
    all_gather x1, waiting for transfers between devices, local(): lax.all_gather(key_rows.reshape(2, group_len, width_now), 'ctx', axis=1,...  68.9 us
    all_gather x1, blocking collectives, local(): lax.all_gather(delta.reshape(2, group_len, head_count), 'ctx', axis=1, ti...  66.3 us
    all_gather x1, blocking collectives, local(): lax.all_gather(log_total.reshape(2, group_len, head_count), 'ctx', axis=1...  56.2 us
    ppermute x2, starting transfers between devices, extended_2(): lax.ppermute(head, axis, [((i + 1) % count, i) for i in range(count)])  18.4 us
    dynamic_slice x16, local copies, waits for them, and re-layouts, inner(): lax.dynamic_slice_in_dim(grad_block, begin, step_rows, 1)  17.2 us
    dynamic_slice x16, local copies, waits for them, and re-layouts, inner(): lax.dynamic_slice_in_dim(value_block, begin, step_rows, 1)  15.7 us
    dynamic_slice x16, local copies, waits for them, and re-layouts, inner(): lax.dynamic_slice_in_dim(key_block, begin, step_rows, 1)  15.6 us
  transfers between devices with their start and end apart: 9, of which 6 were waited for; matrix products, arithmetic and copies ran while one was open for 25% of the time, Pallas kernels for 0%

commit v1 on v0

--- a/solution.py
+++ b/solution.py
@@ -301,7 +301,15 @@
         initial,
         (
             lax.all_gather(key_rows.reshape(2, group_len, width_now), "ctx", axis=1, tiled=True),
-            lax.all_gather(value_rows.reshape(2, group_len, width_now), "ctx", axis=1, tiled=True),
+            jnp.concatenate(
+                lax.all_to_all(
+                    jnp.stack([value_rows.reshape(2, group_len, width_now)] * lax.axis_size("ctx")),
+                    "ctx",
+                    0,
+                    0,
+                ),
+                axis=1,
+            ),
         ),
         jnp.int32(0),
     )

time: 529 us -> 558 us (1.055)
  the two profiles are of different devices: /device:TPU:4 before, /device:TPU:6 now
where the time goes in v1:
time: 558 us; the launch traced here: 555 us
  waiting for transfers between devices  192 us (34%)
  blocking collectives  122 us (22%)
  matrix products  91.3 us (16%)
  local copies, waits for them, and re-layouts  79.3 us (14%)
  starting transfers between devices  33.2 us (6%)
  between operations  16.9 us (3%)
  other arithmetic  15.2 us (3%)
    all_to_all x1, waiting for transfers between devices, local(): lax.all_to_all(jnp.stack([value_rows.reshape(2, group_len, width_now)] *...  111 us
    all_gather x1, blocking collectives, local(): lax.all_gather(delta.reshape(2, group_len, head_count), 'ctx', axis=1, ti...  66.4 us
    all_gather x1, waiting for transfers between devices, local(): lax.all_gather(key_rows.reshape(2, group_len, width_now), 'ctx', axis=1,...  62.3 us
    all_gather x1, blocking collectives, local(): lax.all_gather(log_total.reshape(2, group_len, head_count), 'ctx', axis=1...  56.1 us
    ppermute x2, starting transfers between devices, extended_2(): lax.ppermute(head, axis, [((i + 1) % count, i) for i in range(count)])  18.4 us
    dynamic_slice x16, local copies, waits for them, and re-layouts, inner(): lax.dynamic_slice_in_dim(grad_block, begin, step_rows, 1)  17.2 us
    dynamic_slice x16, local copies, waits for them, and re-layouts, inner(): lax.dynamic_slice_in_dim(value_block, begin, step_rows, 1)  15.7 us
    dynamic_slice x16, local copies, waits for them, and re-layouts, inner(): lax.dynamic_slice_in_dim(key_block, begin, step_rows, 1)  15.6 us
  transfers between devices with their start and end apart: 9, of which 6 were waited for; matrix products, arithmetic and copies ran while one was open for 24% of the time, Pallas kernels for 0%

profile of v1, /device:TPU:6, one launch (start us, length us, event | category | flops | bytes accessed | tf_op | source)
XLA Modules:
  0.0 555.2 jit_solution(3535764443972508873)
XLA Ops:
  7.9 13.8 %collective-permute-start.1 = (bf16[2,3,256]{2,0,1:T(2,128)(2,1)S(1)}, bf16[2,3,256]{2,0,1:T(2,128)(2,1)S(1)}, u32[]{:S(2)}, u32[]{:S(2)}) collective-permute-start(bf16[2,3,256]{2,0,1:T(2,128)(2,1)S(1)} %slice.223), channel_id=1, source_target_pairs={{8,0},{16,8},{24,16},{32,24},{40,32},{48,40},{56,48},{64,56},{72,6... | collective-permute-start | bytes 9224 | tf_op jit(solution)/shard_map/ppermute | solution.py:20
  26.9 1.9 collective-permute-start
  28.9 6.8 %collective-permute-done = bf16[2,3,256]{2,0,1:T(2,128)(2,1)S(1)} collective-permute-done((bf16[2,3,256]{2,0,1:T(2,128)(2,1)S(1)}, bf16[2,3,256]{2,0,1:T(2,128)(2,1)S(1)}, u32[]{:S(2)}, u32[]{:S(2)}) %collective-permute-start) | collective-permute-done | bytes 3104 | tf_op jit(solution)/shard_map/ppermute | solution.py:18
  36.6 1.5 copy.314
  38.1 4.8 all-to-all-start.1
  43.6 2.8 all-to-all-done.1
  46.4 2.5 stack.6
  48.9 5.8 %all-to-all-start = ((bf16[64,2,64,256]{3,2,1,0:T(8,128)(2,1)}), bf16[64,2,64,256]{3,2,1,0:T(8,128)(2,1)}, u32[]{:S(2)}, u32[]{:S(2)}) async-start(bf16[64,2,64,256]{3,2,1,0:T(8,128)(2,1)} %stack.6), calls=%async_computation | async-start | bytes 8388608 | tf_op jit(solution)/shard_map/all_to_all | solution.py:305
  55.5 111.0 %all-to-all-done = bf16[64,2,64,256]{3,2,1,0:T(8,128)(2,1)} async-done(((bf16[64,2,64,256]{3,2,1,0:T(8,128)(2,1)}), bf16[64,2,64,256]{3,2,1,0:T(8,128)(2,1)}, u32[]{:S(2)}, u32[]{:S(2)}) %all-to-all-start) | async-done | bytes 4194336 | tf_op jit(solution)/shard_map/all_to_all | solution.py:305
  166.5 4.7 copy.213
  171.2 62.3 %all-gather.4.cloned.1.call-done = bf16[2,4096,256]{2,1,0:T(8,128)(2,1)} async-done(((bf16[2,64,256]{2,1,0:T(8,128)(2,1)}), bf16[2,4096,256]{2,1,0:T(8,128)(2,1)}) %all-gather.4.cloned.1.call-update) | async-done | bytes 4194320 | tf_op jit(solution)/shard_map/all_gather | solution.py:303
  233.5 114.1 %while.56 = (s32[]{:T(128)}, f32[2,64]{1,0:T(2,128)S(1)}, f32[2,64]{1,0:T(2,128)S(1)}, f32[64,2,128]{2,0,1:T(8,128)S(1)}, f32[64,2,128]{2,0,1:T(8,128)S(1)}, /*i...) while((s32[]{:T(128)}, f32[2,64]{1,0:T(2,128)S(1)}, ...), condition=%wide.region_5.6_spmd.clone, body=%wide.region_0.5_spmd.clone.sunk | while | flops 308006656 | bytes 15106853 | solution.py:162
  235.9 1.0 constant_dynamic-slice_fusion.8
  240.7 1.0 constant_dynamic-slice_fusion.7
  243.1 1.0 constant_dynamic-slice_fusion.8
  247.8 1.0 constant_dynamic-slice_fusion.7
  250.2 1.0 constant_dynamic-slice_fusion.8
  254.9 1.0 constant_dynamic-slice_fusion.7
  257.3 1.0 constant_dynamic-slice_fusion.8
  262.1 1.0 constant_dynamic-slice_fusion.7
  264.5 1.0 constant_dynamic-slice_fusion.8
  269.2 1.0 constant_dynamic-slice_fusion.7
  271.6 1.0 constant_dynamic-slice_fusion.8
  276.3 1.0 constant_dynamic-slice_fusion.7
  278.7 1.0 constant_dynamic-slice_fusion.8
  283.4 1.0 constant_dynamic-slice_fusion.7
  285.9 1.0 constant_dynamic-slice_fusion.8
  290.6 1.0 constant_dynamic-slice_fusion.7
  293.0 1.0 constant_dynamic-slice_fusion.8
  300.1 1.0 constant_dynamic-slice_fusion.8
  304.8 1.0 constant_dynamic-slice_fusion.7
  307.3 1.0 constant_dynamic-slice_fusion.8
  312.0 1.0 constant_dynamic-slice_fusion.7
  314.4 1.0 constant_dynamic-slice_fusion.8
  321.5 1.0 constant_dynamic-slice_fusion.8
  328.7 1.0 constant_dynamic-slice_fusion.8
  335.8 1.0 constant_dynamic-slice_fusion.8
  340.5 1.0 constant_dynamic-slice_fusion.7
  342.9 1.0 constant_dynamic-slice_fusion.8
  349.2 66.4 %all_gather.19 = f32[2,4096,2]{2,0,1:T(2,128)} all-gather(f32[2,64,2]{2,0,1:T(2,128)S(1)} %copy.227), channel_id=1, replica_groups=mesh['ctx'=64,'head'=8] {'ctx'}, dimensions={1}, use_global_device_ids=true | all-gather | bytes 66560 | tf_op jit(solution)/shard_map/all_gather | solution.py:349
  415.6 5.2 copy.231
  421.0 56.1 %all_gather.17 = f32[2,4096,2]{2,0,1:T(2,128)} all-gather(f32[2,64,2]{2,0,1:T(2,128)S(1)} %copy.224), channel_id=1, replica_groups=mesh['ctx'=64,'head'=8] {'ctx'}, dimensions={1}, use_global_device_ids=true | all-gather | bytes 66560 | tf_op jit(solution)/shard_map/all_gather | solution.py:348
  477.1 5.1 copy.229
  483.0 49.3 %while.57 = (s32[]{:T(128)}, f32[64,2,128]{2,0,1:T(8,128)S(1)}, f32[64,2,128]{2,0,1:T(8,128)S(1)}, f32[64,2,128]{2,0,1:T(8,128)S(1)}, f32[64,2,128]{2,0,1:T(8,12...) while((s32[]{:T(128)}, f32[64,2,128]{2,0,1:T(8,128)S(1)}, ...), condition=%wide.region_9.10_spmd.clone, body=%wide.region_8.9_spmd.clone.sunk | while | flops 135473152 | bytes 6612724 | solution.py:250
  483.0 1.1 constant_dynamic-slice_fusion.9
  486.1 1.1 constant_dynamic-slice_fusion.9
  489.1 1.1 constant_dynamic-slice_fusion.9
  492.2 1.1 constant_dynamic-slice_fusion.9
  495.3 1.1 constant_dynamic-slice_fusion.9
  498.4 1.1 constant_dynamic-slice_fusion.9
  501.5 1.1 constant_dynamic-slice_fusion.9
  504.6 1.1 constant_dynamic-slice_fusion.9
  507.7 1.1 constant_dynamic-slice_fusion.9
  510.7 1.1 constant_dynamic-slice_fusion.9
  513.8 1.1 constant_dynamic-slice_fusion.9
  516.9 1.1 constant_dynamic-slice_fusion.9
  520.0 1.1 constant_dynamic-slice_fusion.9
  523.1 1.1 constant_dynamic-slice_fusion.9
  526.2 1.1 constant_dynamic-slice_fusion.9
  529.3 1.1 constant_dynamic-slice_fusion.9
  532.8 4.6 collective-permute-start.2
  537.5 1.3 collective-permute-done.2
  538.8 2.3 collective-permute-start.3
  541.1 6.8 %collective-permute-done.3 = f32[2,3,256]{2,0,1:T(2,128)S(1)} collective-permute-done((f32[2,3,256]{2,0,1:T(2,128)S(1)}, f32[2,3,256]{2,0,1:T(2,128)S(1)}, u32[]{:S(2)}, u32[]{:S(2)}) %collective-permute-start.3) | collective-permute-done | bytes 6176 | tf_op jit(solution)/shard_map/ppermute | solution.py:18
  (848 shorter events, 124.2 us)
Async XLA Ops:
  7.2 226.4 %all-gather.4.cloned.1.call-start = ((), (), s32[]{:S(2)}) async-start(), calls=%async_computation.2 | async-start | bytes 4259840 | tf_op jit(solution)/shard_map/all_gather | solution.py:303
  7.9 18.3 %collective-permute-start.1 = (bf16[2,3,256]{2,0,1:T(2,128)(2,1)S(1)}, bf16[2,3,256]{2,0,1:T(2,128)(2,1)S(1)}, u32[]{:S(2)}, u32[]{:S(2)}) collective-permute-start(bf16[2,3,256]{2,0,1:T(2,128)(2,1)S(1)} %slice.223), channel_id=1, source_target_pairs={{8,0},{16,8},{24,16},{32,24},{40,32},{48,40},{56,48},{64,56},{72,6... | collective-permute-start | bytes 9224 | tf_op jit(solution)/shard_map/ppermute | solution.py:20
  26.9 8.8 %collective-permute-start = (bf16[2,3,256]{2,0,1:T(2,128)(2,1)S(1)}, bf16[2,3,256]{2,0,1:T(2,128)(2,1)S(1)}, u32[]{:S(2)}, u32[]{:S(2)}) collective-permute-start(bf16[2,3,256]{2,0,1:T(2,128)(2,1)S(1)} %get-tuple-element.1180), channel_id=1, source_target_pairs={{0,8},{8,16},{16,24},{24,32},{32,40},{40,48},{48,56},{56,64},{64,7... | collective-permute-start | bytes 9224 | tf_op jit(solution)/shard_map/ppermute | solution.py:18
  38.1 8.3 %all-to-all-start.1 = ((bf16[16,8,256]{2,0,1:T(8,128)(2,1)}), bf16[16,8,256]{2,0,1:T(8,128)(2,1)S(1)}, u32[]{:S(2)}, u32[]{:S(2)}) async-start(bf16[16,8,256]{2,0,1:T(8,128)(2,1)} %bitcast.119), calls=%async_computation.1 | async-start | bytes 131072 | tf_op jit(solution)/shard_map/all_to_all | solution.py:270
  42.9 440.1 %all-gather.6.cloned.1.call-start = ((), (), s32[]{:S(2)}) async-start(), calls=%async_computation.3 | async-start | bytes 4259840 | tf_op jit(solution)/shard_map/all_gather | solution.py:336
  46.4 8.7 %copy-start = (bf16[16,8,256]{2,0,1:T(8,128)(2,1)}, bf16[16,8,256]{2,0,1:T(8,128)(2,1)S(1)}, u32[]{:S(2)}) copy-start(bf16[16,8,256]{2,0,1:T(8,128)(2,1)S(1)} %all-to-all-done.1) | copy-start | bytes 196612
  48.9 6.0 %copy-start.1 = (bf16[128,1,256]{2,0,1:T(8,128)(2,1)S(1)}, bf16[128,1,256]{2,0,1:T(8,128)(2,1)}, u32[]{:S(2)}) copy-start(bf16[128,1,256]{2,0,1:T(8,128)(2,1)} %get-tuple-element.1178) | copy-start | bytes 196612
  48.9 6.0 %copy-start.2 = (bf16[128,1,256]{2,0,1:T(8,128)(2,1)S(1)}, bf16[128,1,256]{2,0,1:T(8,128)(2,1)}, u32[]{:S(2)}) copy-start(bf16[128,1,256]{2,0,1:T(8,128)(2,1)} %get-tuple-element.1177) | copy-start | bytes 196612
  48.9 117.6 %all-to-all-start = ((bf16[64,2,64,256]{3,2,1,0:T(8,128)(2,1)}), bf16[64,2,64,256]{3,2,1,0:T(8,128)(2,1)}, u32[]{:S(2)}, u32[]{:S(2)}) async-start(bf16[64,2,64,256]{3,2,1,0:T(8,128)(2,1)} %stack.6), calls=%async_computation | async-start | bytes 8388608 | tf_op jit(solution)/shard_map/all_to_all | solution.py:305
  54.7 428.3 %all-gather.8.cloned.1.call-start = ((), (), s32[]{:S(2)}) async-start(), calls=%async_computation.4 | async-start | bytes 4259840 | tf_op jit(solution)/shard_map/all_gather | solution.py:342
  55.5 178.1 %copy-start.3 = (s32[128]{0:T(128)S(1)}, s32[128]{0:T(128)}, u32[]{:S(2)}) copy-start(s32[128]{0:T(128)} %param.9) | copy-start | bytes 1540
  532.8 5.9 %collective-permute-start.2 = (f32[2,3,256]{2,0,1:T(2,128)S(1)}, f32[2,3,256]{2,0,1:T(2,128)S(1)}, u32[]{:S(2)}, u32[]{:S(2)}) collective-permute-start(f32[2,3,256]{2,0,1:T(2,128)S(1)} %pad_maximum_fusion.8), channel_id=1, source_target_pairs={{8,0},{16,8},{24,16},{32,24},{40,32},{48,40},{56,48},{64,56},{72,6... | collective-permute-start | bytes 18440 | tf_op jit(solution)/shard_map/ppermute | solution.py:20
  538.8 9.1 %collective-permute-start.3 = (f32[2,3,256]{2,0,1:T(2,128)S(1)}, f32[2,3,256]{2,0,1:T(2,128)S(1)}, u32[]{:S(2)}, u32[]{:S(2)}) collective-permute-start(f32[2,3,256]{2,0,1:T(2,128)S(1)} %get-tuple-element.1145), channel_id=1, source_target_pairs={{0,8},{8,16},{16,24},{24,32},{32,40},{40,48},{48,56},{56,64},{64,7... | collective-permute-start | bytes 18440 | tf_op jit(solution)/shard_map/ppermute | solution.py:18
Sparse Core Ops, SparseCore 0:
  36.7 196.7 all-gather.3
  236.6 84.1 all-gather.5
  323.9 92.1 all-gather.7
